TPU v7x, 128 devices: a whole 4x4x4 slice. The times are simulated.
128 devices in a mesh: ctx: 16 (over y_lo, z, core), tp: 8 (over y_hi, x).
Axes of the slice: x: 4, y: 4 (y_hi: 2, y_lo: 2; y = y_hi * 2 + y_lo), z: 4, core: 2. Of those that a mesh axis runs over, the one named last changes fastest.
Arguments:
- tokens: bfloat16 [4096, 16384], P('tp', 'ctx'), may hold values from -6 to 6
- in_weight: bfloat16 [3, 4096, 4096], P(None, 'ctx', 'tp'), may hold values from -0.09375 to 0.09375
- short_taps: float32 [3, 4096, 3], P(None, 'tp'), may hold values from -3 to 3
- long_filter: float32 [4096, 16384], P('tp', 'ctx'), may hold values from -2 to 2
- skip_gain: float32 [4096], P('tp'), may hold values from -4 to 4
- out_weight: bfloat16 [4096, 4096], P('tp', 'ctx'), may hold values from -0.125 to 0.125
Outputs:
- layer_out: bfloat16 [4096, 16384], P('tp', 'ctx')
All inputs are finite; a program needn't handle non-finite values.
Results may differ from a plain program's by a relative error of at most 0.02.
Values may be sent and summed in bfloat16 or wider, within the bound.
A program may use at most 128 MiB of HBM per device.

v0:
```python
import math
import jax
import jax.numpy as jnp
from jax import lax
from jax.sharding import PartitionSpec as P

HIGHEST = lax.Precision.HIGHEST


def passed_along(shard, axis, by):
    count = lax.axis_size(axis)
    pairs = [(i, i + by) for i in range(count) if 0 <= i + by < count]
    return lax.ppermute(shard, axis, pairs)


def factor_length(full_len):
    inner_len = 1
    while inner_len * inner_len * 4 <= full_len and full_len % (inner_len * 2) == 0:
        inner_len = inner_len * 2
    return (inner_len, full_len // inner_len)


def phase_table(rows_count, cols_count, period):
    row_ids = jnp.arange(rows_count, dtype=jnp.int32)[:, None]
    col_ids = jnp.arange(cols_count, dtype=jnp.int32)[None, :]
    angles = (row_ids * col_ids % period).astype(jnp.float32) * (2.0 * math.pi / period)
    return (jnp.cos(angles), jnp.sin(angles))


def make_tables(full_len):
    inner_len, outer_len = factor_length(full_len)
    cos_inner, sin_inner = phase_table(inner_len, inner_len, inner_len)
    cos_outer, sin_outer = phase_table(outer_len // 2, outer_len, outer_len)
    cos_twist, sin_twist = phase_table(outer_len, inner_len, full_len)
    return (cos_inner, sin_inner, cos_outer, sin_outer, cos_twist, sin_twist)


def spectrum(signal, tables):
    cos_inner, sin_inner, cos_outer, sin_outer, cos_twist, sin_twist = tables
    channels = signal.shape[0]
    grid_view = signal.reshape(channels, cos_outer.shape[0], cos_inner.shape[0])
    part_re = jnp.einsum("cmn,mk->ckn", grid_view, cos_outer, precision=HIGHEST)
    part_im = -jnp.einsum("cmn,mk->ckn", grid_view, sin_outer, precision=HIGHEST)
    twist_re = part_re * cos_twist + part_im * sin_twist
    twist_im = part_im * cos_twist - part_re * sin_twist
    freq_re = jnp.einsum("ckn,nj->ckj", twist_re, cos_inner, precision=HIGHEST) + jnp.einsum(
        "ckn,nj->ckj", twist_im, sin_inner, precision=HIGHEST
    )
    freq_im = jnp.einsum("ckn,nj->ckj", twist_im, cos_inner, precision=HIGHEST) - jnp.einsum(
        "ckn,nj->ckj", twist_re, sin_inner, precision=HIGHEST
    )
    return (freq_re, freq_im)


def spectrum_back(freq_re, freq_im, tables):
    cos_inner, sin_inner, cos_outer, sin_outer, cos_twist, sin_twist = tables
    mix_re = jnp.einsum("ckj,jn->ckn", freq_re, cos_inner, precision=HIGHEST) - jnp.einsum(
        "ckj,jn->ckn", freq_im, sin_inner, precision=HIGHEST
    )
    mix_im = jnp.einsum("ckj,jn->ckn", freq_im, cos_inner, precision=HIGHEST) + jnp.einsum(
        "ckj,jn->ckn", freq_re, sin_inner, precision=HIGHEST
    )
    turn_re = mix_re * cos_twist - mix_im * sin_twist
    turn_im = mix_im * cos_twist + mix_re * sin_twist
    channels = freq_re.shape[0]
    length = cos_outer.shape[0] * cos_inner.shape[0]
    norm_factor = 1.0 / (cos_outer.shape[1] * cos_inner.shape[0])
    real_out = jnp.einsum("ckn,mk->cmn", turn_re, cos_outer, precision=HIGHEST) - jnp.einsum(
        "ckn,mk->cmn", turn_im, sin_outer, precision=HIGHEST
    )
    real_out = real_out.reshape(channels, length) * norm_factor
    return real_out


def per_device(tokens, in_weight, short_taps, long_filter, skip_gain, out_weight):
    steps_dev = tokens.shape[1]
    filter_groups = lax.all_to_all(
        long_filter.astype(jnp.bfloat16), "ctx", split_axis=0, concat_axis=1, tiled=True
    ).astype(long_filter.dtype)
    features_all = lax.all_gather(tokens, "tp", axis=0, tiled=True)
    sources = (features_all,)
    shard_rows = lax.all_gather(in_weight, "ctx", axis=1, tiled=True)
    results = tuple(
        (
            jnp.einsum("sic,it->sct", shard_rows, source, preferred_element_type=jnp.float32)
            for source in sources
        )
    )
    projected = results[0]
    before = passed_along(projected[:, :, steps_dev - 2 :], "ctx", 1)
    prev_one = jnp.concatenate([before[:, :, 1:], projected[:, :, :-1]], axis=2)
    prev_two = jnp.concatenate([before, projected[:, :, :-2]], axis=2)
    mixed_short = (
        short_taps[:, :, 0:1] * projected
        + short_taps[:, :, 1:2] * prev_one
        + short_taps[:, :, 2:3] * prev_two
    )
    gated_rows = (mixed_short[1] * mixed_short[2]).astype(jnp.bfloat16)
    signal = lax.all_to_all(gated_rows, "ctx", split_axis=0, concat_axis=1, tiled=True)
    tables = make_tables(2 * signal.shape[1])
    sig_re, sig_im = spectrum(signal.astype(jnp.float32), tables)
    fil_re, fil_im = spectrum(filter_groups, tables)
    prod_re = sig_re * fil_re - sig_im * fil_im
    prod_im = sig_re * fil_im + sig_im * fil_re
    long_rows = spectrum_back(prod_re, prod_im, tables)
    long_rows = long_rows.astype(jnp.bfloat16)
    returned = lax.all_to_all(long_rows, "ctx", split_axis=1, concat_axis=0, tiled=True)
    hidden = (
        (returned.astype(jnp.float32) + skip_gain[:, None] * gated_rows.astype(jnp.float32))
        * mixed_short[0]
    ).astype(jnp.bfloat16)
    whole_out = lax.all_gather(out_weight, "ctx", axis=1, tiled=True)
    return lax.psum_scatter(
        jnp.einsum("cd,ct->dt", whole_out, hidden, preferred_element_type=jnp.float32).astype(
            jnp.bfloat16
        ),
        "tp",
        scatter_dimension=0,
        tiled=True,
    )


def solution(mesh):
    placed = (
        P("tp", "ctx"),
        P(None, "ctx", "tp"),
        P(None, "tp", None),
        P("tp", "ctx"),
        P("tp"),
        P("tp", "ctx"),
    )
    return jax.shard_map(
        per_device, mesh=mesh, in_specs=placed, out_specs=P("tp", "ctx"), check_vma=False
    )
```

profile of v0, /device:TPU:1, one launch (start us, length us, event | category | flops | bytes accessed | tf_op | source)
XLA Modules:
  0.0 480.2 jit_solution(12676117775673328608)
XLA Ops:
  10.8 7.8 %all-to-all-start.1 = ((bf16[16,32,1024]{2,1,0:T(8,128)(2,1)}), bf16[16,32,1024]{2,1,0:T(8,128)(2,1)S(1)}, u32[]{:S(2)}, u32[]{:S(2)}) async-start(bf16[16,32,1024]{2,1,0:T(8,128)(2,1)} %bitcast.11), calls=%async_computation.1 | async-start | bytes 2097152 | tf_op jit(solution)/shard_map/all_to_all | solution.py:77
  20.0 19.7 %all-to-all-done.1 = bf16[16,32,1024]{2,1,0:T(8,128)(2,1)S(1)} async-done(((bf16[16,32,1024]{2,1,0:T(8,128)(2,1)}), bf16[16,32,1024]{2,1,0:T(8,128)(2,1)S(1)}, u32[]{:S(2)}, u32[]{:S(2)}) %all-to-all-start.1) | async-done | bytes 1048608 | tf_op jit(solution)/shard_map/all_to_all | solution.py:77
  47.4 5.6 %fusion.6 = f32[32,256,128]{2,1,0:T(8,128)} fusion(f32[256,32,128]{2,0,1:T(8,128)S(1)} %fusion.64, f32[256,32,128]{2,0,1:T(8,128)S(1)} %fusion.60, f32[256,128]{1,0:T(8,128)S(1)} %get-tuple-element.12, f32[256,128]{1,0:T(8,128)S(1)} %get-tuple-element.13), kind=kOutput, calls=%fused_computation.9 | convolution fusion | flops 1615036416 | bytes 12845056 | tf_op jit(solution)/shard_map/ckn,nj->ckj/dot_general | solution.py:46
  53.0 74.5 %all-gather.6.cloned.1.call-done = bf16[4096,1024]{1,0:T(8,128)(2,1)} async-done(((bf16[512,1024]{1,0:T(8,128)(2,1)}), bf16[4096,1024]{1,0:T(8,128)(2,1)}) %all-gather.6.cloned.1.call-update) | async-done | bytes 8388624 | tf_op jit(solution)/shard_map/all_gather | solution.py:80
  127.5 79.9 %all-gather.4.cloned.1.call-done = bf16[3,4096,512]{1,2,0:T(8,128)(2,1)} async-done(((bf16[3,256,512]{1,2,0:T(8,128)(2,1)}), bf16[3,4096,512]{1,2,0:T(8,128)(2,1)}) %all-gather.4.cloned.1.call-update) | async-done | bytes 12582928 | tf_op jit(solution)/shard_map/all_gather | solution.py:82
  207.3 16.7 %fusion = f32[3,512,1024]{2,1,0:T(8,128)S(1)} fusion(bf16[3,4096,512]{1,2,0:T(8,128)(2,1)} %all-gather.4.cloned.1.call-done, bf16[4096,1024]{1,0:T(8,128)(2,1)} %all-gather.6.cloned.1.call-done), kind=kOutput, calls=%fused_computation | convolution fusion | flops 12884901888 | bytes 27262976 | tf_op jit(solution)/shard_map/sic,it->sct/dot_general | solution.py:85
  230.0 8.5 %fusion.34 = f32[32,256,128]{2,1,0:T(8,128)} fusion(f32[32,256,128]{2,1,0:T(8,128)} %fusion.6, f32[256,32,128]{2,0,1:T(8,128)} %copy-done, f32[256,32,128]{2,0,1:T(8,128)} %copy-done.2, f32[256,128]{1,0:T(8,128)S(1)} %get-tuple-element.12, f32[256,128]{1,0:T(8,128)S(1)} %get-tuple-element.13), kind=kOutput, calls=%fused_computation.39 | convolution fusion | flops 1616084992 | bytes 17039360 | tf_op jit(solution)/shard_map/ckn,nj->ckj/dot_general | solution.py:46
  239.1 9.3 %fusion.3 = f32[3,512,1024]{2,1,0:T(8,128)S(1)} fusion(f32[3,512,1023]{2,1,0:T(8,128)} %bitcast.120, f32[3,512,1]{2,1,0:T(8,128)S(1)} %copy.27, f32[3,512,1022]{2,1,0:T(8,128)} %bitcast.121, f32[3,512,2]{2,1,0:T(8,128)S(1)} %copy.28, f32[3,512,1024]{2,1,0:T(8,128)} %copy-done.4, f32[3,512]{1,0:T(4,128)S(1)} %get-tuple-element.10, ...), kind=kLoop, calls=%fused_computation.5 | loop fusion | flops 11010048 | bytes 25184256 | tf_op jit(solution)/shard_map/add | solution.py:94
  252.3 4.5 all-to-all-start
  256.9 6.8 %fusion.4 = f32[32,256,128]{2,1,0:T(8,128)S(1)} fusion(f32[256,32,128]{2,0,1:T(8,128)} %copy-done, f32[256,32,128]{2,0,1:T(8,128)} %copy-done.2, f32[256,128]{1,0:T(8,128)S(1)} %get-tuple-element.12, f32[256,128]{1,0:T(8,128)S(1)} %get-tuple-element.13), kind=kOutput, calls=%fused_computation.7 | convolution fusion | flops 1615036416 | bytes 12845056 | tf_op jit(solution)/shard_map/ckn,nj->ckj/dot_general | solution.py:49
  263.7 5.7 %fusion.37 = f32[32,256,128]{2,1,0:T(8,128)} fusion(f32[32,256,128]{2,1,0:T(8,128)S(1)} %fusion.4, f32[256,32,128]{2,0,1:T(8,128)S(1)} %copy-done.1, f32[256,32,128]{2,0,1:T(8,128)S(1)} %copy-done.3, f32[256,128]{1,0:T(8,128)S(1)} %get-tuple-element.12, f32[256,128]{1,0:T(8,128)S(1)} %get-tuple-element.13), kind=kOutput, calls=%fused_computation.40 | convolution fusion | flops 1616084992 | bytes 17039360 | tf_op jit(solution)/shard_map/ckn,nj->ckj/dot_general | solution.py:49
  278.8 4.3 fusion.14
  283.2 5.5 %fusion.12 = f32[32,256,128]{2,1,0:T(8,128)S(1)} fusion(f32[256,32,128]{2,0,1:T(8,128)S(1)} %fusion.66, f32[256,32,128]{2,0,1:T(8,128)S(1)} %fusion.62, f32[256,128]{1,0:T(8,128)} %copy-done.6, f32[256,128]{1,0:T(8,128)} %copy-done.9), kind=kOutput, calls=%fused_computation.15 | convolution fusion | flops 1615036416 | bytes 12845056 | tf_op jit(solution)/shard_map/ckn,nj->ckj/dot_general | solution.py:49
  288.7 5.7 %fusion.28 = f32[32,256,128]{2,1,0:T(8,128)} fusion(f32[32,256,128]{2,1,0:T(8,128)S(1)} %fusion.14, f32[256,32,128]{2,0,1:T(8,128)S(1)} %fusion.66, f32[256,32,128]{2,0,1:T(8,128)S(1)} %fusion.62, f32[256,128]{1,0:T(8,128)S(1)} %copy-done.7, f32[256,128]{1,0:T(8,128)S(1)} %copy-done.10), kind=kOutput, calls=%fused_computation.37 | convolution fusion | flops 1616084992 | bytes 17039360 | tf_op jit(solution)/shard_map/ckn,nj->ckj/dot_general | solution.py:46
  294.4 8.4 %multiply_add_fusion = (f32[32,256,128]{2,1,0:T(8,128)S(1)}, f32[32,256,128]{2,1,0:T(8,128)S(1)}) fusion(f32[32,256,128]{2,1,0:T(8,128)} %fusion.34, f32[32,256,128]{2,1,0:T(8,128)} %fusion.28, f32[32,256,128]{2,1,0:T(8,128)} %fusion.37, f32[32,256,128]{2,1,0:T(8,128)S(1)} %fusion.12, f32[256,128]{1,0:T(8,128)} %copy-done.6, ...), kind=kOutput, calls=%fused_computation.31 | convolution fusion | flops 1622376448 | bytes 33816576 | tf_op jit(solution)/shard_map/ckn,nj->ckj/dot_general | solution.py:49
  302.8 3.7 fusion.86
  306.5 3.7 fusion.84
  310.1 3.7 convolution_subtract_fusion
  313.8 3.9 convolution_add_fusion
  321.0 3.4 fusion.50
  325.5 19.1 %all_to_all.39 = bf16[32,16,1024]{2,0,1:T(8,128)(2,1)S(1)} all-to-all(bf16[32,16,1024]{2,0,1:T(8,128)(2,1)S(1)} %copy.35), channel_id=1, replica_groups=mesh['ctx'=16,'tp'=8] {'ctx'}, dimensions={1} | all-to-all | bytes 2097152 | tf_op jit(solution)/shard_map/all_to_all | solution.py:107
  344.6 3.4 fusion.41
  348.0 9.0 %convert_bitcast_fusion = bf16[4096,1024]{0,1:T(8,128)(2,1)} fusion(bf16[512,1024]{1,0:T(8,128)(2,1)S(1)} %fusion.41, bf16[512,4096]{1,0:T(8,128)(2,1)} %all-gather.8.cloned.1.call-done), kind=kOutput, calls=%fused_computation.2 | convolution fusion | flops 4299161600 | bytes 13631488 | tf_op jit(solution)/shard_map/cd,ct->dt/dot_general | solution.py:114
  357.0 113.9 %reduce-scatter.2.cloned.1.call-done = bf16[512,1024]{0,1:T(8,128)(2,1)} async-done(((bf16[4096,1024]{0,1:T(8,128)(2,1)}), bf16[512,1024]{0,1:T(8,128)(2,1)}) %reduce-scatter.2.cloned.1.call-update) | async-done | bytes 1048592 | tf_op jit(solution)/shard_map/reduce_scatter | solution.py:113
  (66 shorter events, 39.8 us)
Async XLA Ops:
  6.5 3.1 copy-start.12
  6.5 120.9 %all-gather.6.cloned.1.call-start = ((), (), s32[]{:S(2)}) async-start(), calls=%async_computation.5 | async-start | bytes 9437184 | tf_op jit(solution)/shard_map/all_gather | solution.py:80
  7.3 12.1 %copy-start.13 = (f32[3,512,3]{1,2,0:T(4,128)S(1)}, f32[3,512,3]{1,2,0:T(4,128)}, u32[]{:S(2)}) copy-start(f32[3,512,3]{1,2,0:T(4,128)} %param.8) | copy-start | bytes 55300
  7.3 200.1 %all-gather.4.cloned.1.call-start = ((), (), s32[]{:S(2)}) async-start(), calls=%async_computation.4 | async-start | bytes 13369344 | tf_op jit(solution)/shard_map/all_gather | solution.py:82
  10.8 28.8 %all-to-all-start.1 = ((bf16[16,32,1024]{2,1,0:T(8,128)(2,1)}), bf16[16,32,1024]{2,1,0:T(8,128)(2,1)S(1)}, u32[]{:S(2)}, u32[]{:S(2)}) async-start(bf16[16,32,1024]{2,1,0:T(8,128)(2,1)} %bitcast.11), calls=%async_computation.1 | async-start | bytes 2097152 | tf_op jit(solution)/shard_map/all_to_all | solution.py:77
  18.6 329.4 %all-gather.8.cloned.1.call-start = ((), (), s32[]{:S(2)}) async-start(), calls=%async_computation.6 | async-start | bytes 4456448 | tf_op jit(solution)/shard_map/all_gather | solution.py:112
  20.0 258.9 %copy-start.6 = (f32[256,128]{1,0:T(8,128)}, f32[256,128]{1,0:T(8,128)S(1)}, u32[]{:S(2)}) copy-start(f32[256,128]{1,0:T(8,128)S(1)} %get-tuple-element.12) | copy-start | bytes 393220
  20.0 258.9 %copy-start.9 = (f32[256,128]{1,0:T(8,128)}, f32[256,128]{1,0:T(8,128)S(1)}, u32[]{:S(2)}) copy-start(f32[256,128]{1,0:T(8,128)S(1)} %get-tuple-element.13) | copy-start | bytes 393220
  43.1 2.4 copy-start
  45.4 2.0 copy-start.2
  224.1 2.6 copy-start.4
  227.2 11.3 %collective-permute-start = (f32[3,512,2]{1,2,0:T(2,128)S(1)}, f32[3,512,2]{1,2,0:T(2,128)S(1)}, u32[]{:S(2)}, u32[]{:S(2)}) collective-permute-start(f32[3,512,2]{1,2,0:T(2,128)S(1)} %copy.26), channel_id=1, source_target_pairs={{0,8},{8,16},{16,24},{24,32},{32,40},{40,48},{48,56},{56,64},{64,7... | collective-permute-start | bytes 36872 | tf_op jit(solution)/shard_map/ppermute | solution.py:13
  248.4 2.6 copy-start.5
  252.3 20.3 %all-to-all-start = ((bf16[16,32,1024]{2,1,0:T(8,128)(2,1)}), bf16[16,32,1024]{2,1,0:T(8,128)(2,1)S(1)}, u32[]{:S(2)}, u32[]{:S(2)}) async-start(bf16[16,32,1024]{2,1,0:T(8,128)(2,1)} %bitcast.3), calls=%async_computation | async-start | bytes 2097152 | tf_op jit(solution)/shard_map/all_to_all | solution.py:99
  256.9 214.1 %reduce-scatter.2.cloned.1.call-start = ((), (), s32[]{:S(2)}) async-start(), calls=%async_computation.7 | async-start | bytes 9437184 | tf_op jit(solution)/shard_map/reduce_scatter | solution.py:113
  256.9 6.8 %copy-start.1 = (f32[256,32,128]{2,0,1:T(8,128)S(1)}, f32[256,32,128]{2,0,1:T(8,128)}, u32[]{:S(2)}) copy-start(f32[256,32,128]{2,0,1:T(8,128)} %copy-done) | copy-start | bytes 12582916
  256.9 6.8 %copy-start.3 = (f32[256,32,128]{2,0,1:T(8,128)S(1)}, f32[256,32,128]{2,0,1:T(8,128)}, u32[]{:S(2)}) copy-start(f32[256,32,128]{2,0,1:T(8,128)} %copy-done.2) | copy-start | bytes 12582916
  283.2 5.5 %copy-start.7 = (f32[256,128]{1,0:T(8,128)S(1)}, f32[256,128]{1,0:T(8,128)}, u32[]{:S(2)}) copy-start(f32[256,128]{1,0:T(8,128)} %copy-done.6) | copy-start | bytes 393220
  283.2 5.5 %copy-start.10 = (f32[256,128]{1,0:T(8,128)S(1)}, f32[256,128]{1,0:T(8,128)}, u32[]{:S(2)}) copy-start(f32[256,128]{1,0:T(8,128)} %copy-done.9) | copy-start | bytes 393220
  313.8 3.9 copy-start.8
  313.8 3.9 copy-start.11
  324.4 20.2 %copy-start.14 = (f32[512]{0:T(512)S(1)}, f32[512]{0:T(512)}, u32[]{:S(2)}) copy-start(f32[512]{0:T(512)} %param.10) | copy-start | bytes 6148
Sparse Core Ops, SparseCore 0:
  9.7 117.7 all-gather.5
  129.1 78.2 all-gather.3
  209.0 45.4 all-gather.7
  357.2 113.7 reduce-scatter.1
where the time goes:
time: 489 us; the launch traced here: 480 us
  waiting for transfers between devices  293 us (60%)
  matrix products  107 us (22%)
  blocking collectives  19.1 us (4%)
  local copies, waits for them, and re-layouts  16.7 us (3%)
  other arithmetic  15.6 us (3%)
  starting transfers between devices  15.3 us (3%)
  between operations  14 us (3%)
    reduce_scatter x1, waiting for transfers between devices, per_device(): lax.psum_scatter(jnp.einsum('cd,ct->dt', whole_out, hidden, preferred_ele...  114 us
    all_gather x1, waiting for transfers between devices, per_device(): shard_rows = lax.all_gather(in_weight, 'ctx', axis=1, tiled=True)  79.9 us
    all_gather x1, waiting for transfers between devices, per_device(): features_all = lax.all_gather(tokens, 'tp', axis=0, tiled=True)  74.5 us
    all_to_all x1, waiting for transfers between devices, per_device(): lax.all_to_all(long_filter.astype(jnp.bfloat16), 'ctx', split_axis=0, con...  19.7 us
    all_to_all x1, blocking collectives, per_device(): lax.all_to_all(long_rows, 'ctx', split_axis=1, concat_axis=0, tiled=True)  19.1 us
    dot_general x1, matrix products, per_device(): jnp.einsum('sic,it->sct', shard_rows, source, preferred_element_type=jnp....  16.7 us
    dot_general x2, matrix products, spectrum(): jnp.einsum('ckn,nj->ckj', twist_re, sin_inner, precision=HIGHEST)  14.1 us
    dot_general x2, matrix products, spectrum(): jnp.einsum('ckn,nj->ckj', twist_re, cos_inner, precision=HIGHEST)  14.1 us
  transfers between devices with their start and end apart: 7, of which 5 were waited for; matrix products, arithmetic and copies ran while one was open for 25% of the time, Pallas kernels for 0%

commit v1 on v0

--- a/solution.py
+++ b/solution.py
@@ -104,7 +104,10 @@
     prod_im = sig_re * fil_im + sig_im * fil_re
     long_rows = spectrum_back(prod_re, prod_im, tables)
     long_rows = long_rows.astype(jnp.bfloat16)
-    returned = lax.all_to_all(long_rows, "ctx", split_axis=1, concat_axis=0, tiled=True)
+    returned = jnp.concatenate(
+        lax.all_to_all(jnp.stack(jnp.split(long_rows, lax.axis_size("ctx"), axis=1)), "ctx", 0, 0),
+        axis=0,
+    )
     hidden = (
         (returned.astype(jnp.float32) + skip_gain[:, None] * gated_rows.astype(jnp.float32))
         * mixed_short[0]

time: 489 us -> 500 us (1.022)
  blocking collectives: 19.1 us -> 0 us
  waiting for transfers between devices: 293 us -> 308 us
  local copies, waits for them, and re-layouts: 16.7 us -> 26.3 us
    all_to_all x1 -> x0, blocking collectives: 19.1 us -> none  [per_device(): lax.all_to_all(long_rows, 'ctx', split_axis=1, concat_axis=0, tiled=True)]
    all_to_all x0 -> x1, waiting for transfers between devices: none -> 15.6 us  [per_device(): lax.all_to_all(jnp.stack(jnp.split(long_rows, lax.axis_size('ctx'), axis=...]
    unnamed x33 -> x49, local copies, waits for them, and re-layouts: 9.58 us -> 19.7 us
  transfers between devices with their start and end apart: 7 -> 8, of which waited for: 5 -> 6; matrix products, arithmetic and copies ran while one was open for 25% -> 26% of each run, Pallas kernels for 0% -> 0%
where the time goes in v1:
time: 500 us; the launch traced here: 491 us
  waiting for transfers between devices  308 us (62%)
  matrix products  110 us (22%)
  local copies, waits for them, and re-layouts  26.3 us (5%)
  starting transfers between devices  19.8 us (4%)
  between operations  14 us (3%)
  other arithmetic  12.2 us (2%)
    reduce_scatter x1, waiting for transfers between devices, per_device(): lax.psum_scatter(jnp.einsum('cd,ct->dt', whole_out, hidden, preferred_ele...  114 us
    all_gather x1, waiting for transfers between devices, per_device(): shard_rows = lax.all_gather(in_weight, 'ctx', axis=1, tiled=True)  79.9 us
    all_gather x1, waiting for transfers between devices, per_device(): features_all = lax.all_gather(tokens, 'tp', axis=0, tiled=True)  74.4 us
    unnamed x49, local copies, waits for them, and re-layouts  19.7 us
    all_to_all x1, waiting for transfers between devices, per_device(): lax.all_to_all(long_filter.astype(jnp.bfloat16), 'ctx', split_axis=0, con...  19.7 us
    dot_general x2, matrix products, spectrum(): jnp.einsum('ckn,nj->ckj', twist_re, sin_inner, precision=HIGHEST)  16.9 us
    dot_general x1, matrix products, per_device(): jnp.einsum('sic,it->sct', shard_rows, source, preferred_element_type=jnp....  16.7 us
    all_to_all x1, waiting for transfers between devices, per_device(): lax.all_to_all(jnp.stack(jnp.split(long_rows, lax.axis_size('ctx'), axis=...  15.6 us
  transfers between devices with their start and end apart: 8, of which 6 were waited for; matrix products, arithmetic and copies ran while one was open for 26% of the time, Pallas kernels for 0%

profile of v1, /device:TPU:1, one launch (start us, length us, event | category | flops | bytes accessed | tf_op | source)
XLA Modules:
  0.0 490.6 jit_solution(2270216014508966554)
XLA Ops:
  10.8 7.8 %all-to-all-start.1 = ((bf16[16,32,1024]{2,1,0:T(8,128)(2,1)}), bf16[16,32,1024]{2,1,0:T(8,128)(2,1)S(1)}, u32[]{:S(2)}, u32[]{:S(2)}) async-start(bf16[16,32,1024]{2,1,0:T(8,128)(2,1)} %bitcast.11), calls=%async_computation.1 | async-start | bytes 2097152 | tf_op jit(solution)/shard_map/all_to_all | solution.py:77
  20.0 19.7 %all-to-all-done.1 = bf16[16,32,1024]{2,1,0:T(8,128)(2,1)S(1)} async-done(((bf16[16,32,1024]{2,1,0:T(8,128)(2,1)}), bf16[16,32,1024]{2,1,0:T(8,128)(2,1)S(1)}, u32[]{:S(2)}, u32[]{:S(2)}) %all-to-all-start.1) | async-done | bytes 1048608 | tf_op jit(solution)/shard_map/all_to_all | solution.py:77
  47.5 5.6 %fusion.4 = f32[32,256,128]{2,1,0:T(8,128)} fusion(f32[256,32,128]{2,0,1:T(8,128)S(1)} %fusion.64, f32[256,32,128]{2,0,1:T(8,128)S(1)} %fusion.60, f32[256,128]{1,0:T(8,128)S(1)} %get-tuple-element.12, f32[256,128]{1,0:T(8,128)S(1)} %get-tuple-element.13), kind=kOutput, calls=%fused_computation.7 | convolution fusion | flops 1615036416 | bytes 12845056 | tf_op jit(solution)/shard_map/ckn,nj->ckj/dot_general | solution.py:49
  53.1 74.4 %all-gather.6.cloned.1.call-done = bf16[4096,1024]{1,0:T(8,128)(2,1)} async-done(((bf16[512,1024]{1,0:T(8,128)(2,1)}), bf16[4096,1024]{1,0:T(8,128)(2,1)}) %all-gather.6.cloned.1.call-update) | async-done | bytes 8388624 | tf_op jit(solution)/shard_map/all_gather | solution.py:80
  127.5 79.9 %all-gather.4.cloned.1.call-done = bf16[3,4096,512]{1,2,0:T(8,128)(2,1)} async-done(((bf16[3,256,512]{1,2,0:T(8,128)(2,1)}), bf16[3,4096,512]{1,2,0:T(8,128)(2,1)}) %all-gather.4.cloned.1.call-update) | async-done | bytes 12582928 | tf_op jit(solution)/shard_map/all_gather | solution.py:82
  207.3 16.7 %fusion = f32[3,512,1024]{2,1,0:T(8,128)S(1)} fusion(bf16[3,4096,512]{1,2,0:T(8,128)(2,1)} %all-gather.4.cloned.1.call-done, bf16[4096,1024]{1,0:T(8,128)(2,1)} %all-gather.6.cloned.1.call-done), kind=kOutput, calls=%fused_computation | convolution fusion | flops 12884901888 | bytes 27262976 | tf_op jit(solution)/shard_map/sic,it->sct/dot_general | solution.py:85
  230.0 8.5 %fusion.37 = f32[32,256,128]{2,1,0:T(8,128)} fusion(f32[32,256,128]{2,1,0:T(8,128)} %fusion.4, f32[256,32,128]{2,0,1:T(8,128)} %copy-done.2, f32[256,32,128]{2,0,1:T(8,128)} %copy-done, f32[256,128]{1,0:T(8,128)S(1)} %get-tuple-element.12, f32[256,128]{1,0:T(8,128)S(1)} %get-tuple-element.13), kind=kOutput, calls=%fused_computation.40 | convolution fusion | flops 1616084992 | bytes 17039360 | tf_op jit(solution)/shard_map/ckn,nj->ckj/dot_general | solution.py:49
  239.1 9.3 %fusion.3 = f32[3,512,1024]{2,1,0:T(8,128)S(1)} fusion(f32[3,512,1023]{2,1,0:T(8,128)} %bitcast.188, f32[3,512,1]{2,1,0:T(8,128)S(1)} %copy.25, f32[3,512,1022]{2,1,0:T(8,128)} %bitcast.189, f32[3,512,2]{2,1,0:T(8,128)S(1)} %copy.26, f32[3,512,1024]{2,1,0:T(8,128)} %copy-done.4, f32[3,512]{1,0:T(4,128)S(1)} %get-tuple-element.10, ...), kind=kLoop, calls=%fused_computation.5 | loop fusion | flops 11010048 | bytes 25184256 | tf_op jit(solution)/shard_map/add | solution.py:94
  252.4 4.5 all-to-all-start
  256.9 6.8 %fusion.6 = f32[32,256,128]{2,1,0:T(8,128)S(1)} fusion(f32[256,32,128]{2,0,1:T(8,128)} %copy-done.2, f32[256,32,128]{2,0,1:T(8,128)} %copy-done, f32[256,128]{1,0:T(8,128)S(1)} %get-tuple-element.12, f32[256,128]{1,0:T(8,128)S(1)} %get-tuple-element.13), kind=kOutput, calls=%fused_computation.9 | convolution fusion | flops 1615036416 | bytes 12845056 | tf_op jit(solution)/shard_map/ckn,nj->ckj/dot_general | solution.py:46
  263.8 5.7 %fusion.34 = f32[32,256,128]{2,1,0:T(8,128)} fusion(f32[32,256,128]{2,1,0:T(8,128)S(1)} %fusion.6, f32[256,32,128]{2,0,1:T(8,128)S(1)} %copy-done.3, f32[256,32,128]{2,0,1:T(8,128)S(1)} %copy-done.1, f32[256,128]{1,0:T(8,128)S(1)} %get-tuple-element.12, f32[256,128]{1,0:T(8,128)S(1)} %get-tuple-element.13), kind=kOutput, calls=%fused_computation.39 | convolution fusion | flops 1616084992 | bytes 17039360 | tf_op jit(solution)/shard_map/ckn,nj->ckj/dot_general | solution.py:46
  278.9 4.3 fusion.14
  283.3 5.5 %fusion.12 = f32[32,256,128]{2,1,0:T(8,128)S(1)} fusion(f32[256,32,128]{2,0,1:T(8,128)S(1)} %fusion.66, f32[256,32,128]{2,0,1:T(8,128)S(1)} %fusion.62, f32[256,128]{1,0:T(8,128)} %copy-done.6, f32[256,128]{1,0:T(8,128)} %copy-done.9), kind=kOutput, calls=%fused_computation.15 | convolution fusion | flops 1615036416 | bytes 12845056 | tf_op jit(solution)/shard_map/ckn,nj->ckj/dot_general | solution.py:49
  288.8 5.7 %fusion.28 = f32[32,256,128]{2,1,0:T(8,128)} fusion(f32[32,256,128]{2,1,0:T(8,128)S(1)} %fusion.14, f32[256,32,128]{2,0,1:T(8,128)S(1)} %fusion.66, f32[256,32,128]{2,0,1:T(8,128)S(1)} %fusion.62, f32[256,128]{1,0:T(8,128)S(1)} %copy-done.7, f32[256,128]{1,0:T(8,128)S(1)} %copy-done.10), kind=kOutput, calls=%fused_computation.37 | convolution fusion | flops 1616084992 | bytes 17039360 | tf_op jit(solution)/shard_map/ckn,nj->ckj/dot_general | solution.py:46
  294.6 8.4 %multiply_add_fusion = (f32[32,256,128]{2,1,0:T(8,128)S(1)}, f32[32,256,128]{2,1,0:T(8,128)S(1)}) fusion(f32[32,256,128]{2,1,0:T(8,128)} %fusion.34, f32[32,256,128]{2,1,0:T(8,128)} %fusion.28, f32[32,256,128]{2,1,0:T(8,128)} %fusion.37, f32[32,256,128]{2,1,0:T(8,128)S(1)} %fusion.12, f32[256,128]{1,0:T(8,128)} %copy-done.6, ...), kind=kOutput, calls=%fused_computation.31 | convolution fusion | flops 1622376448 | bytes 33816576 | tf_op jit(solution)/shard_map/ckn,nj->ckj/dot_general | solution.py:49
  303.0 3.8 fusion.100
  306.8 3.7 fusion.102
  310.4 3.8 convolution_add_fusion
  314.3 3.9 convolution_subtract_fusion
  321.5 3.4 multiply_convert_fusion
  335.6 4.3 all-to-all-start.2
  340.2 15.6 %all-to-all-done.2 = bf16[16,32,1024]{2,1,0:T(8,128)(2,1)S(1)} async-done(((bf16[16,32,1024]{2,1,0:T(8,128)(2,1)}), bf16[16,32,1024]{2,1,0:T(8,128)(2,1)S(1)}, u32[]{:S(2)}, u32[]{:S(2)}) %all-to-all-start.2) | async-done | bytes 1048608 | tf_op jit(solution)/shard_map/all_to_all | solution.py:108
  355.8 11.3 %convert_bitcast_fusion = bf16[4096,1024]{0,1:T(8,128)(2,1)} fusion(bf16[512,4096]{1,0:T(8,128)(2,1)} %all-gather.8.cloned.1.call-done, f32[3,512,1024]{2,1,0:T(8,128)} %copy-done.5, bf16[512,1024]{1,0:T(8,128)(2,1)S(1)} %bitcast.209, bf16[1,512,1024]{2,1,0:T(8,128)(2,1)} %fusion.42, f32[512]{0:T(512)S(1)} %copy-done.14), kind=kOutput, calls=%fused_computation.2 | convolution fusion | flops 4302307328 | bytes 16779264 | tf_op jit(solution)/shard_map/cd,ct->dt/dot_general | solution.py:117
  367.1 114.3 %reduce-scatter.2.cloned.1.call-done = bf16[512,1024]{0,1:T(8,128)(2,1)} async-done(((bf16[4096,1024]{0,1:T(8,128)(2,1)}), bf16[512,1024]{0,1:T(8,128)(2,1)}) %reduce-scatter.2.cloned.1.call-update) | async-done | bytes 1048592 | tf_op jit(solution)/shard_map/reduce_scatter | solution.py:116
  (81 shorter events, 49.7 us)
Async XLA Ops:
  6.5 3.1 copy-start.12
  6.5 120.9 %all-gather.6.cloned.1.call-start = ((), (), s32[]{:S(2)}) async-start(), calls=%async_computation.5 | async-start | bytes 9437184 | tf_op jit(solution)/shard_map/all_gather | solution.py:80
  7.3 12.1 %copy-start.13 = (f32[3,512,3]{1,2,0:T(4,128)S(1)}, f32[3,512,3]{1,2,0:T(4,128)}, u32[]{:S(2)}) copy-start(f32[3,512,3]{1,2,0:T(4,128)} %param.8) | copy-start | bytes 55300
  7.3 200.1 %all-gather.4.cloned.1.call-start = ((), (), s32[]{:S(2)}) async-start(), calls=%async_computation.4 | async-start | bytes 13369344 | tf_op jit(solution)/shard_map/all_gather | solution.py:82
  10.8 28.9 %all-to-all-start.1 = ((bf16[16,32,1024]{2,1,0:T(8,128)(2,1)}), bf16[16,32,1024]{2,1,0:T(8,128)(2,1)S(1)}, u32[]{:S(2)}, u32[]{:S(2)}) async-start(bf16[16,32,1024]{2,1,0:T(8,128)(2,1)} %bitcast.11), calls=%async_computation.1 | async-start | bytes 2097152 | tf_op jit(solution)/shard_map/all_to_all | solution.py:77
  18.6 321.6 %all-gather.8.cloned.1.call-start = ((), (), s32[]{:S(2)}) async-start(), calls=%async_computation.6 | async-start | bytes 4456448 | tf_op jit(solution)/shard_map/all_gather | solution.py:115
  20.0 258.9 %copy-start.6 = (f32[256,128]{1,0:T(8,128)}, f32[256,128]{1,0:T(8,128)S(1)}, u32[]{:S(2)}) copy-start(f32[256,128]{1,0:T(8,128)S(1)} %get-tuple-element.12) | copy-start | bytes 393220
  20.0 258.9 %copy-start.9 = (f32[256,128]{1,0:T(8,128)}, f32[256,128]{1,0:T(8,128)S(1)}, u32[]{:S(2)}) copy-start(f32[256,128]{1,0:T(8,128)S(1)} %get-tuple-element.13) | copy-start | bytes 393220
  43.1 2.4 copy-start
  45.4 2.0 copy-start.2
  224.1 2.6 copy-start.4
  227.2 11.3 %collective-permute-start = (f32[3,512,2]{1,2,0:T(2,128)S(1)}, f32[3,512,2]{1,2,0:T(2,128)S(1)}, u32[]{:S(2)}, u32[]{:S(2)}) collective-permute-start(f32[3,512,2]{1,2,0:T(2,128)S(1)} %copy.24), channel_id=1, source_target_pairs={{0,8},{8,16},{16,24},{24,32},{32,40},{40,48},{48,56},{56,64},{64,7... | collective-permute-start | bytes 36872 | tf_op jit(solution)/shard_map/ppermute | solution.py:13
  248.4 2.7 copy-start.5
  252.4 20.4 %all-to-all-start = ((bf16[16,32,1024]{2,1,0:T(8,128)(2,1)}), bf16[16,32,1024]{2,1,0:T(8,128)(2,1)S(1)}, u32[]{:S(2)}, u32[]{:S(2)}) async-start(bf16[16,32,1024]{2,1,0:T(8,128)(2,1)} %bitcast.3), calls=%async_computation | async-start | bytes 2097152 | tf_op jit(solution)/shard_map/all_to_all | solution.py:99
  256.9 6.8 %copy-start.1 = (f32[256,32,128]{2,0,1:T(8,128)S(1)}, f32[256,32,128]{2,0,1:T(8,128)}, u32[]{:S(2)}) copy-start(f32[256,32,128]{2,0,1:T(8,128)} %copy-done) | copy-start | bytes 12582916
  256.9 6.8 %copy-start.3 = (f32[256,32,128]{2,0,1:T(8,128)S(1)}, f32[256,32,128]{2,0,1:T(8,128)}, u32[]{:S(2)}) copy-start(f32[256,32,128]{2,0,1:T(8,128)} %copy-done.2) | copy-start | bytes 12582916
  283.3 5.5 %copy-start.7 = (f32[256,128]{1,0:T(8,128)S(1)}, f32[256,128]{1,0:T(8,128)}, u32[]{:S(2)}) copy-start(f32[256,128]{1,0:T(8,128)} %copy-done.6) | copy-start | bytes 393220
  283.3 5.5 %copy-start.10 = (f32[256,128]{1,0:T(8,128)S(1)}, f32[256,128]{1,0:T(8,128)}, u32[]{:S(2)}) copy-start(f32[256,128]{1,0:T(8,128)} %copy-done.9) | copy-start | bytes 393220
  314.3 3.9 copy-start.8
  314.3 3.9 copy-start.11
  324.9 30.9 %copy-start.14 = (f32[512]{0:T(512)S(1)}, f32[512]{0:T(512)}, u32[]{:S(2)}) copy-start(f32[512]{0:T(512)} %param.10) | copy-start | bytes 6148
  335.6 20.2 %all-to-all-start.2 = ((bf16[16,32,1024]{2,1,0:T(8,128)(2,1)}), bf16[16,32,1024]{2,1,0:T(8,128)(2,1)S(1)}, u32[]{:S(2)}, u32[]{:S(2)}) async-start(bf16[16,32,1024]{2,1,0:T(8,128)(2,1)} %fusion.78), calls=%async_computation.2 | async-start | bytes 2097152 | tf_op jit(solution)/shard_map/all_to_all | solution.py:108
  339.9 141.5 %reduce-scatter.2.cloned.1.call-start = ((), (), s32[]{:S(2)}) async-start(), calls=%async_computation.7 | async-start | bytes 9437184 | tf_op jit(solution)/shard_map/reduce_scatter | solution.py:116
Sparse Core Ops, SparseCore 0:
  9.7 117.7 all-gather.5
  129.1 78.2 all-gather.3
  209.0 45.4 all-gather.7
  367.2 114.1 reduce-scatter.1
